TPU v7x, 512 devices: a whole 4x4x16 slice. The times are simulated.
512 devices in a mesh: tm: 16 (over y, x), seq: 32 (over z, core).
Axes of the slice: x: 4, y: 4, z: 16, core: 2. Of those that a mesh axis runs over, the one named last changes fastest.
Arguments:
- latent_start: float32 [2048, 64], P('seq'), may hold values from -6 to 6
- noise: float32 [16, 2048, 64], P('tm', 'seq'), may hold values from -6 to 6
- step_index: int32 [16], P('tm'), may hold values from 0 to 49
- camera_ids: int32 [2048], P('seq'), may hold values from 0 to 5
- embed_in: bfloat16 [64, 2048], replicated, may hold values from -0.75 to 0.75
- time_table: float32 [50, 2048], replicated, may hold values from -6 to 6
- camera_table: float32 [6, 2048], replicated, may hold values from -6 to 6
- norm_gain: float32 [2048], replicated, may hold values from 0.25 to 1.75
- qkv_weight: bfloat16 [2048, 32, 192], P(None, 'seq'), as said below
- final_gain: float32 [2048], replicated, may hold values from 0.25 to 1.75
- out_weight: bfloat16 [2048, 64], replicated, may hold values from -0.125 to 0.125
- step_sizes: float32 [50], replicated, may hold values from 0.1 to 0.4
- noise_scales: float32 [50], replicated, may hold values from 0.1 to 0.4
Outputs:
- latents_out: float32 [16, 2048, 64], P('tm', 'seq')
Inputs may be any that keep to these rules, and one draw needn't show every extreme that they name: `qkv_weight`: every entry lies within 26 / sqrt(2048) in magnitude.
All inputs are finite; a program needn't handle non-finite values.
Results may differ from a plain program's by a relative error of at most 0.002.
Values may be sent and summed in bfloat16 or wider, within the bound.
A program may use at most 64 MiB of HBM per device.

v0:
```python
import jax
import jax.numpy as jnp
from jax import lax
from jax.sharding import PartitionSpec as P


def entering(part, axis, combine, identity):
    place = lax.axis_index(axis)
    gathered = lax.all_gather(part, axis)
    state = jnp.zeros_like(part) + jnp.asarray(identity, part.dtype)

    def one(hop, state):
        return combine(state, lax.dynamic_index_in_dim(gathered, hop, 0, False))

    return lax.fori_loop(0, place, one, state)


def rms_scale(value, gain):
    return value * lax.rsqrt(jnp.mean(value * value, axis=-1, keepdims=True) + 1e-06) * gain


def camera_lookup(ids, camera_table):
    total = jnp.zeros((ids.shape[0], camera_table.shape[1]), jnp.float32)
    for camera in range(camera_table.shape[0]):
        total = total + jnp.where(ids[:, None] == camera, camera_table[camera][None, :], 0.0)
    return total


def attend(qkv):
    total = qkv.shape[0]
    hsize = qkv.shape[1] // 3
    query = qkv[:, :hsize]
    keys = qkv[:, hsize : 2 * hsize]
    values = qkv[:, 2 * hsize :]
    block = 512
    blocks = query.reshape(total // block, block, hsize)

    def one_block(rows):
        scores = jnp.dot(rows, keys.T, preferred_element_type=jnp.float32) * hsize ** (-0.5)
        peak = jnp.max(scores, axis=-1, keepdims=True)
        expo = jnp.exp(scores - peak)
        probs = (expo / jnp.sum(expo, axis=-1, keepdims=True)).astype(jnp.bfloat16)
        return jnp.dot(probs, values, preferred_element_type=jnp.float32).astype(jnp.bfloat16)

    return lax.map(one_block, blocks).reshape(total, hsize)


def body(
    latent_start,
    noise,
    step_index,
    camera_ids,
    embed_in,
    time_table,
    camera_table,
    norm_gain,
    qkv_weight,
    final_gain,
    out_weight,
    step_sizes,
    noise_scales,
):
    tau = step_index[0]
    time_row = lax.dynamic_slice_in_dim(time_table, tau, 1, 0)
    step_coef = lax.dynamic_slice_in_dim(step_sizes, tau, 1, 0)[0]
    noise_coef = lax.dynamic_slice_in_dim(noise_scales, tau, 1, 0)[0]
    noise_local = noise[0]
    local_heads = qkv_weight.shape[1]
    own_camera = camera_lookup(camera_ids, camera_table)

    def add_terms(earlier, later):
        return earlier + later

    latent = latent_start
    earlier = jnp.zeros_like(latent_start)
    term = jnp.zeros_like(latent_start)
    for sweep_number in range(2):
        rounded = latent.astype(jnp.bfloat16)
        hidden = (
            jnp.dot(rounded, embed_in, preferred_element_type=jnp.float32) + time_row + own_camera
        )
        normed = rms_scale(hidden, norm_gain).astype(jnp.bfloat16)
        qkv = jnp.einsum(
            "td,dhk->thk",
            lax.all_gather(normed, "seq", axis=0, tiled=True),
            qkv_weight,
            preferred_element_type=jnp.float32,
        ).astype(jnp.bfloat16)
        head_out = jax.vmap(attend, in_axes=1, out_axes=1)(qkv)
        head_out = head_out.reshape(head_out.shape[0], local_heads * head_out.shape[2])
        joined = lax.all_to_all(head_out, "seq", split_axis=0, concat_axis=1, tiled=True)
        mixed = rms_scale(hidden + joined.astype(jnp.float32), final_gain).astype(jnp.bfloat16)
        drift = jnp.dot(mixed, out_weight, preferred_element_type=jnp.float32)
        sweep_term = step_coef * drift + noise_coef * noise_local
        sweep_earlier = entering(sweep_term, "tm", add_terms, jnp.zeros_like(sweep_term))
        earlier = sweep_earlier
        term = sweep_term
        latent = latent_start + earlier
    return (latent_start + (earlier + term))[None]


def solution(mesh):
    in_specs = (
        P("seq", None),
        P("tm", "seq", None),
        P("tm"),
        P("seq"),
        P(),
        P(),
        P(),
        P(),
        P(None, "seq", None),
        P(),
        P(),
        P(),
        P(),
    )
    out_specs = P("tm", "seq", None)
    return jax.shard_map(body, mesh=mesh, in_specs=in_specs, out_specs=out_specs, check_vma=False)
```

profile of v0, /device:TPU:24, one launch (start us, length us, event | category | flops | bytes accessed | tf_op | source)
XLA Modules:
  0.0 331.2 jit_solution(3454476610416154654)
XLA Ops:
  7.3 1.1 fusion.37
  8.4 0.7 broadcast_compare_fusion.5
  9.1 0.8 constant_dynamic-slice_fusion
  9.9 1.5 multiply_reduce_fusion.5
  11.4 1.5 multiply_convert_fusion.3
  13.0 83.9 %all-gather.5.cloned.1.call-done = bf16[2048,2048]{1,0:T(8,128)(2,1)} async-done(((bf16[64,2048]{1,0:T(8,128)(2,1)}), bf16[2048,2048]{1,0:T(8,128)(2,1)}) %all-gather.5.cloned.1.call-update) | async-done | bytes 8388624 | tf_op jit(solution)/shard_map/all_gather | solution.py:85
  96.9 6.3 %fusion.24 = bf16[2048,1,192]{0,2,1:T(8,128)(2,1)S(1)} fusion(bf16[2048,2048]{1,0:T(8,128)(2,1)} %all-gather.5.cloned.1.call-done, bf16[2048,1,192]{0,2,1:T(8,128)(2,1)S(1)} %copy-done), kind=kOutput, calls=%fused_computation.34 | convolution fusion | flops 1611005952 | bytes 9961472 | tf_op jit(solution)/shard_map/td,dhk->thk/dot_general | solution.py:83
  103.3 0.3 copy.42
  103.6 0.3 copy.31
  103.8 0.3 copy.32
  104.2 11.1 %while.40 = (s32[]{:T(128)}, bf16[4,1,512,64]{2,3,1,0:T(8,128)(2,1)S(1)}, bf16[4,1,512,64]{3,2,1,0:T(8,128)(2,1)S(1)}, bf16[1,2048,64]{2,1,0:T(8,128)(2,1)S(1)}, bf16[1,2048,64]{2,1,0:T(8,128)(2,1)S(1)}, /*index=5*/s32[]{:T(128)}) while((s32[]{:T(128)}, bf16[4,1,512,64]{2,3,1,0:T(8,128)(2,1)S(1)}, bf16[4,1,512,64]{3,2,1,0:T(8,128)(2,1)S(1)}, ...), condition=%wide.region_4.5_spmd, body=%wide.region_1.4_spmd.sunk | while | flops 277904384 | bytes 13838413 | solution.py:45
  104.2 0.8 multiply_reduce_fusion.8
  105.0 0.8 fusion.51
  105.8 1.1 fusion.52
  107.0 0.8 multiply_reduce_fusion.8
  107.8 0.8 fusion.51
  108.6 1.1 fusion.52
  109.8 0.8 multiply_reduce_fusion.8
  110.6 0.8 fusion.51
  111.4 1.1 fusion.52
  112.6 0.8 multiply_reduce_fusion.8
  113.3 0.8 fusion.51
  114.2 1.1 fusion.52
  115.6 0.3 all_to_all.20
  116.1 1.1 reshape.135
  117.2 7.9 %all-to-all-start = ((bf16[32,2,2048]{2,1,0:T(2,128)(2,1)}), bf16[32,2,2048]{2,1,0:T(2,128)(2,1)S(1)}, u32[]{:S(2)}, u32[]{:S(2)}) async-start(bf16[32,2,2048]{2,1,0:T(2,128)(2,1)} %reshape.135), calls=%async_computation | async-start | bytes 524288 | tf_op jit(solution)/shard_map/all_to_all | solution.py:91
  125.1 0.7 dynamic_slice.23
  125.8 0.6 dynamic_slice.25
  126.4 21.4 %all-to-all-done = bf16[32,2,2048]{2,1,0:T(2,128)(2,1)S(1)} async-done(((bf16[32,2,2048]{2,1,0:T(2,128)(2,1)}), bf16[32,2,2048]{2,1,0:T(2,128)(2,1)S(1)}, u32[]{:S(2)}, u32[]{:S(2)}) %all-to-all-start) | async-done | bytes 262176 | tf_op jit(solution)/shard_map/all_to_all | solution.py:91
  147.8 0.4 reshape.136
  148.3 0.3 copy.43
  148.8 1.6 fusion.29
  150.4 23.6 %all-gather = f32[1024,64]{1,0:T(8,128)S(1)} all-gather(f32[64,64]{1,0:T(8,128)S(1)} %fusion.29), channel_id=2, replica_groups=mesh['tm'=16,'seq'=32] {'tm'}, dimensions={0}, use_global_device_ids=true | all-gather | bytes 278528 | tf_op jit(solution)/shard_map/all_gather | solution.py:9
  174.0 0.7 while.41
  174.7 1.5 multiply_reduce_fusion.3
  176.2 0.8 multiply_convert_fusion.1
  177.1 69.2 %all-gather.7.cloned.1.call-done = bf16[2048,2048]{1,0:T(8,128)(2,1)} async-done(((bf16[64,2048]{1,0:T(8,128)(2,1)}), bf16[2048,2048]{1,0:T(8,128)(2,1)}) %all-gather.7.cloned.1.call-update) | async-done | bytes 8388624 | tf_op jit(solution)/shard_map/all_gather | solution.py:85
  246.3 6.3 %fusion.25 = bf16[2048,1,192]{0,2,1:T(8,128)(2,1)S(1)} fusion(bf16[2048,2048]{1,0:T(8,128)(2,1)} %all-gather.7.cloned.1.call-done, bf16[2048,1,192]{0,2,1:T(8,128)(2,1)S(1)} %copy-done), kind=kOutput, calls=%fused_computation.35 | convolution fusion | flops 1611005952 | bytes 9961472 | tf_op jit(solution)/shard_map/td,dhk->thk/dot_general | solution.py:83
  252.7 0.3 copy.44
  252.9 0.3 copy.37
  253.2 0.3 copy.38
  253.5 11.1 %while.42 = (s32[]{:T(128)}, bf16[4,1,512,64]{2,3,1,0:T(8,128)(2,1)S(1)}, bf16[4,1,512,64]{3,2,1,0:T(8,128)(2,1)S(1)}, bf16[1,2048,64]{2,1,0:T(8,128)(2,1)S(1)}, bf16[1,2048,64]{2,1,0:T(8,128)(2,1)S(1)}, /*index=5*/s32[]{:T(128)}) while((s32[]{:T(128)}, bf16[4,1,512,64]{2,3,1,0:T(8,128)(2,1)S(1)}, bf16[4,1,512,64]{3,2,1,0:T(8,128)(2,1)S(1)}, ...), condition=%wide.region_12.13_spmd, body=%wide.region_9.12_spmd.sunk | while | flops 277904384 | bytes 13838413 | solution.py:45
  253.6 0.8 multiply_reduce_fusion.9
  254.3 0.8 fusion.54
  255.2 1.1 fusion.55
  256.3 0.8 multiply_reduce_fusion.9
  257.1 0.8 fusion.54
  258.0 1.1 fusion.55
  259.1 0.8 multiply_reduce_fusion.9
  259.9 0.8 fusion.54
  260.7 1.1 fusion.55
  261.9 0.8 multiply_reduce_fusion.9
  262.7 0.8 fusion.54
  263.5 1.1 fusion.55
  264.9 0.3 all_to_all.22
  265.4 1.1 reshape.137
  266.5 7.7 %all-to-all-start.1 = ((bf16[32,2,2048]{2,1,0:T(2,128)(2,1)}), bf16[32,2,2048]{2,1,0:T(2,128)(2,1)S(1)}, u32[]{:S(2)}, u32[]{:S(2)}) async-start(bf16[32,2,2048]{2,1,0:T(2,128)(2,1)} %reshape.137), calls=%async_computation.1 | async-start | bytes 524288 | tf_op jit(solution)/shard_map/all_to_all | solution.py:91
  274.3 22.8 %all-to-all-done.1 = bf16[32,2,2048]{2,1,0:T(2,128)(2,1)S(1)} async-done(((bf16[32,2,2048]{2,1,0:T(2,128)(2,1)}), bf16[32,2,2048]{2,1,0:T(2,128)(2,1)S(1)}, u32[]{:S(2)}, u32[]{:S(2)}) %all-to-all-start.1) | async-done | bytes 262176 | tf_op jit(solution)/shard_map/all_to_all | solution.py:91
  297.0 0.4 reshape.138
  297.5 0.3 copy.45
  298.0 1.6 fusion.28
  299.6 23.6 %all-gather.1 = f32[1024,64]{1,0:T(8,128)S(1)} all-gather(f32[64,64]{1,0:T(8,128)S(1)} %fusion.28), channel_id=3, replica_groups=mesh['tm'=16,'seq'=32] {'tm'}, dimensions={0}, use_global_device_ids=true | all-gather | bytes 278528 | tf_op jit(solution)/shard_map/all_gather | solution.py:9
  323.2 0.5 while.43
  323.7 0.6 add_bitcast_fusion
  (62 shorter events, 2.0 us)
Async XLA Ops:
  6.5 90.4 %copy-start = (bf16[2048,1,192]{0,2,1:T(8,128)(2,1)S(1)}, bf16[2048,1,192]{0,2,1:T(8,128)(2,1)}, u32[]{:S(2)}) copy-start(bf16[2048,1,192]{0,2,1:T(8,128)(2,1)} %param.29) | copy-start | bytes 2359300
  6.5 90.4 %all-gather.5.cloned.1.call-start = ((), (), s32[]{:S(2)}) async-start(), calls=%async_computation.2 | async-start | bytes 8650752 | tf_op jit(solution)/shard_map/all_gather | solution.py:85
  104.2 21.0 %copy-start.6 = (f32[50]{0:T(128)S(1)}, f32[50]{0:T(128)}, u32[]{:S(2)}) copy-start(f32[50]{0:T(128)} %param.32) | copy-start | bytes 604
  104.2 21.6 %copy-start.7 = (f32[50]{0:T(128)S(1)}, f32[50]{0:T(128)}, u32[]{:S(2)}) copy-start(f32[50]{0:T(128)} %param.33) | copy-start | bytes 604
  115.5 33.3 %copy-start.1 = (bf16[2048,64]{0,1:T(8,128)(2,1)S(1)}, bf16[2048,64]{0,1:T(8,128)(2,1)}, u32[]{:S(2)}) copy-start(bf16[2048,64]{0,1:T(8,128)(2,1)} %param.31) | copy-start | bytes 786436
  115.6 33.3 %copy-start.2 = (f32[1,64,64]{2,1,0:T(8,128)S(1)}, f32[1,64,64]{2,1,0:T(8,128)}, u32[]{:S(2)}) copy-start(f32[1,64,64]{2,1,0:T(8,128)} %param.22) | copy-start | bytes 49156
  115.6 33.2 %copy-start.4 = (f32[2048]{0:T(1024)S(1)}, f32[2048]{0:T(1024)}, u32[]{:S(2)}) copy-start(f32[2048]{0:T(1024)} %param.30) | copy-start | bytes 24580
  117.2 57.5 %copy-start.5 = (f32[64,64]{1,0:T(8,128)S(1)}, f32[64,64]{1,0:T(8,128)}, u32[]{:S(2)}) copy-start(f32[64,64]{1,0:T(8,128)} %param.21) | copy-start | bytes 49156
  117.2 30.6 %all-to-all-start = ((bf16[32,2,2048]{2,1,0:T(2,128)(2,1)}), bf16[32,2,2048]{2,1,0:T(2,128)(2,1)S(1)}, u32[]{:S(2)}, u32[]{:S(2)}) async-start(bf16[32,2,2048]{2,1,0:T(2,128)(2,1)} %reshape.135), calls=%async_computation | async-start | bytes 524288 | tf_op jit(solution)/shard_map/all_to_all | solution.py:91
  125.1 121.2 %all-gather.7.cloned.1.call-start = ((), (), s32[]{:S(2)}) async-start(), calls=%async_computation.3 | async-start | bytes 8650752 | tf_op jit(solution)/shard_map/all_gather | solution.py:85
  148.3 27.9 %copy-start.3 = (f32[2048]{0:T(1024)S(1)}, f32[2048]{0:T(1024)}, u32[]{:S(2)}) copy-start(f32[2048]{0:T(1024)} %param.28) | copy-start | bytes 24580
  266.5 30.5 %all-to-all-start.1 = ((bf16[32,2,2048]{2,1,0:T(2,128)(2,1)}), bf16[32,2,2048]{2,1,0:T(2,128)(2,1)S(1)}, u32[]{:S(2)}, u32[]{:S(2)}) async-start(bf16[32,2,2048]{2,1,0:T(2,128)(2,1)} %reshape.137), calls=%async_computation.1 | async-start | bytes 524288 | tf_op jit(solution)/shard_map/all_to_all | solution.py:91
Sparse Core Ops, SparseCore 0:
  13.1 83.7 all-gather.4
  177.2 69.0 all-gather.6
where the time goes:
time: 332 us; the launch traced here: 331 us
  waiting for transfers between devices  197 us (59%)
  blocking collectives  47.2 us (14%)
  matrix products  34.2 us (10%)
  starting transfers between devices  15.7 us (5%)
  between operations  14.5 us (4%)
  other arithmetic  11.1 us (3%)
  local copies, waits for them, and re-layouts  10.1 us (3%)
    all_gather x2, waiting for transfers between devices, body(): lax.all_gather(normed, 'seq', axis=0, tiled=True)  153 us
    all_gather x2, blocking collectives, entering(): gathered = lax.all_gather(part, axis)  47.2 us
    all_to_all x2, waiting for transfers between devices, body(): lax.all_to_all(head_out, 'seq', split_axis=0, concat_axis=1, tiled=True)  44.1 us
    all_to_all x2, starting transfers between devices, body(): lax.all_to_all(head_out, 'seq', split_axis=0, concat_axis=1, tiled=True)  15.6 us
    dot_general x2, matrix products, body(): jnp.einsum('td,dhk->thk', lax.all_gather(normed, 'seq', axis=0, tiled=Tru...  12.6 us
    dot_general x8, matrix products, one_block(): jnp.dot(probs, values, preferred_element_type=jnp.float32)  9.19 us
  transfers between devices with their start and end apart: 4, of which 4 were waited for; matrix products, arithmetic and copies ran while one was open for 0% of the time, Pallas kernels for 0%

commit v1 on v0

v1 whole, which is shorter than its diff:
```python
import functools
import math

import jax
import jax.numpy as jnp
from jax import lax
from jax.experimental import pallas as pl
from jax.experimental.pallas import tpu as pltpu
from jax.sharding import PartitionSpec as P

MESH = pl.DeviceIdType.MESH
F32 = jnp.float32
BF16 = jnp.bfloat16
TOK = 64
HALF = 32
CHIPS = 16
STEPS = 16
BLOCK = 512
RELAYS = ((9, 16), (3, 9), (0, 3))


def slot_offset(slot):
    half = slot // 2
    return 8 + half - (slot % 2) * (1 + 2 * half)


def mirror(slot):
    return 0 if slot == 0 else 15 if slot == 15 else slot + 1 if slot % 2 else slot - 1


def dot(a, b):
    return jnp.dot(a, b, preferred_element_type=F32)


def dot_nt(a, b):
    return lax.dot_general(a, b, (((1,), (1,)), ((), ())), preferred_element_type=F32)


def split2(value):
    high = value.astype(BF16)
    return high, (value - high.astype(F32)).astype(BF16)


def split3(value):
    high = value.astype(BF16)
    rest = value - high.astype(F32)
    middle = rest.astype(BF16)
    return high, middle, (rest - middle.astype(F32)).astype(BF16)


def pack(block):
    flipped = block.T
    return jnp.concatenate([flipped[:HALF], flipped[HALF:]], axis=1)


def kernel(
    ls_ref, noise_ref, step_ref, cam_ref, embed_ref, time_ref, camt_ref, ngain_ref, w_ref,
    fgain_ref, wout_ref, sizes_ref, scales_ref,
    out_ref,
    lsp, noisep, gb0, gb1, u, mw, hw, gw, table, ncol, wot, fgt, k2, vt, qt, ht, s0, s1,
    pout, pin, term, prefix,
    gsend, grecv, rsend, rrecv, msend, mrecv, psend, precv, tsend, trecv,
):
    tm, sq = lax.axis_index("tm"), lax.axis_index("seq")
    z, c = sq // 2, sq % 2
    other = 1 - c
    partner = (tm, 2 * z + other)

    def along(offset):
        return (tm, 2 * ((z + offset) % CHIPS) + c)

    barrier = pltpu.get_barrier_semaphore()

    def greet_z(i, carry):
        pl.semaphore_signal(barrier, inc=1, device_id=along(i), device_id_type=MESH)
        return carry

    def greet_tm(i, carry):
        pl.semaphore_signal(
            barrier, inc=1, device_id=((tm + i) % STEPS, sq), device_id_type=MESH
        )
        return carry

    lax.fori_loop(1, CHIPS, greet_z, 0)
    lax.fori_loop(1, STEPS, greet_tm, 0)
    pl.semaphore_signal(barrier, inc=1, device_id=partner, device_id_type=MESH)

    lsp[...] = pack(ls_ref[...])
    gb0[c, 15, 0:HALF, :] = lsp[...].astype(BF16)
    cam = cam_ref[...].astype(F32).astype(BF16)
    gb0[c, 15, HALF:48, :] = jnp.broadcast_to(jnp.concatenate([cam, cam], axis=1), (16, 128))

    pl.semaphore_wait(barrier, CHIPS - 1 + STEPS - 1 + 1)

    def gather_copy(buf, phase, slot):
        return pltpu.make_async_remote_copy(
            src_ref=buf.at[c, 15],
            dst_ref=buf.at[c, mirror(slot)],
            send_sem=gsend.at[phase, slot],
            recv_sem=grecv.at[phase, mirror(slot)],
            device_id=along(slot_offset(slot)),
            device_id_type=MESH,
        )

    def gather_wait(buf, phase, slot):
        return pltpu.make_async_remote_copy(
            src_ref=buf.at[c, 15],
            dst_ref=buf.at[c, slot],
            send_sem=gsend.at[phase, slot],
            recv_sem=grecv.at[phase, slot],
            device_id=along(slot_offset(slot)),
            device_id_type=MESH,
        )

    def relay_copy(buf, phase, index, core):
        first, last = RELAYS[index]
        part = buf.at[core, pl.ds(first, last - first)]
        return pltpu.make_async_remote_copy(
            src_ref=part,
            dst_ref=part,
            send_sem=rsend.at[phase, index],
            recv_sem=rrecv.at[phase, index],
            device_id=partner,
            device_id_type=MESH,
        )

    def gather_start(buf, phase):
        for slot in range(15):
            gather_copy(buf, phase, slot).start()

    def gather_finish(buf, phase):
        for index, (first, last) in enumerate(RELAYS):
            for slot in reversed(range(first, min(last, 15))):
                gather_wait(buf, phase, slot).wait_recv()
            relay_copy(buf, phase, index, c).start()
        for index in range(len(RELAYS)):
            relay_copy(buf, phase, index, other).wait_recv()
        for slot in range(15):
            gather_copy(buf, phase, slot).wait_send()
        for index in range(len(RELAYS)):
            relay_copy(buf, phase, index, c).wait_send()

    def assemble(buf, cameras):
        for side in range(2):
            core = c if side == 0 else other
            for pair in range(8):
                lanes = slice(side * 1024 + pair * 128, side * 1024 + pair * 128 + 128)
                left = buf[core, 2 * pair]
                right = buf[core, 2 * pair + 1]
                low = jnp.concatenate([left[:, :64], right[:, :64]], axis=1)
                high = jnp.concatenate([left[:, 64:], right[:, 64:]], axis=1)
                tile = jnp.concatenate([low[:HALF], high[:HALF]], axis=0)
                u[0:64, lanes] = tile
                u[64:128, lanes] = tile
                u[128:192, lanes] = tile
                if cameras:
                    ids = low[HALF : HALF + 16].astype(F32)
                    row = lax.broadcasted_iota(jnp.int32, (16, 128), 0).astype(F32)
                    one = jnp.where(ids == row, 1.0, 0.0).astype(BF16)
                    u[192:208, lanes] = one
                    u[208:224, lanes] = one
                    u[224:240, lanes] = one

    gather_start(gb0, 0)

    tau = step_ref[0]
    rows = camt_ref[...] + time_ref[pl.ds(tau, 1), :]
    rows = jnp.concatenate([rows, jnp.zeros((10, rows.shape[1]), F32)], axis=0)
    table[...] = rows
    embed = embed_ref[...]
    gain = ngain_ref[...]
    eg_high, eg_low = split2(embed.astype(F32) * gain)
    rg_high, rg_low = split2(rows * gain)
    folded = dot(jnp.concatenate([eg_high, rg_high, eg_low, rg_low], axis=0), w_ref[...])
    fold_x = folded[0:64] + folded[80:144]
    fold_e = folded[64:80] + folded[144:160]
    fx_high = fold_x.astype(BF16).astype(F32)
    fe_high = fold_e.astype(BF16).astype(F32)
    width = fold_x.shape[1]
    stacked = jnp.concatenate(
        [
            fx_high, fold_x - fx_high, jnp.zeros((64, width), F32),
            fe_high, fold_e - fe_high, jnp.zeros((32, width), F32),
        ],
        axis=0,
    )
    mw[c] = stacked.T.astype(BF16)
    exchange = pltpu.make_async_remote_copy(
        src_ref=mw.at[c], dst_ref=mw.at[c], send_sem=msend, recv_sem=mrecv,
        device_id=partner, device_id_type=MESH,
    )
    exchange.start()

    gram = dot_nt(embed, embed)
    r_high, r_middle, r_low = split3(rows)
    cross = 2.0 * (dot_nt(r_low, embed) + dot_nt(r_middle, embed) + dot_nt(r_high, embed))
    g3 = [part.astype(F32) for part in split3(gram)]
    c3 = [part.astype(F32) for part in split3(cross)]
    gw[...] = jnp.concatenate(g3 + c3 + [jnp.zeros((16, 64), F32)], axis=0).T.astype(BF16)
    ncol[...] = jnp.broadcast_to(jnp.sum(rows * rows, axis=1, keepdims=True), ncol.shape)

    columns = pl.ds(pl.multiple_of(z * 128, 128), 128)
    h3 = [part.astype(F32) for part in split3(table[:, columns])]
    hw[...] = jnp.concatenate(
        [embed_ref[:, columns].astype(F32), jnp.zeros((128, 128), F32)]
        + h3
        + [jnp.zeros((16, 128), F32)],
        axis=0,
    ).T.astype(BF16)
    fgt[...] = jnp.broadcast_to(fgain_ref[:, columns], (128, 128)).T
    wot[...] = wout_ref[columns, :].astype(F32).T.astype(BF16)
    noisep[...] = pack(noise_ref[0])
    step_coef = sizes_ref[tau]
    noise_coef = scales_ref[tau]

    u[240:256, :] = jnp.zeros((16, u.shape[1]), BF16)
    vt[:, 64:80, :] = jnp.ones((2, 16, vt.shape[2]), BF16)
    qt[...] = jnp.zeros_like(qt)

    exchange.wait_send()
    pltpu.make_async_remote_copy(
        src_ref=mw.at[other], dst_ref=mw.at[other], send_sem=msend, recv_sem=mrecv,
        device_id=partner, device_id_type=MESH,
    ).wait_recv()
    gather_finish(gb0, 0)
    assemble(gb0, True)

    def project(chunk, own):
        lanes = slice(chunk * BLOCK, chunk * BLOCK + BLOCK)
        part = u[:, lanes]
        mixed = dot(gw[...], part)
        square = jnp.sum(mixed * part[0:64].astype(F32), axis=0, keepdims=True)
        flags = part[192:208].astype(F32)
        square = square + jnp.sum(flags * ncol[:, 0:1], axis=0, keepdims=True)
        scale = lax.rsqrt(jnp.maximum(square, 0.0) * (1.0 / 2048) + 1e-06)
        keys = dot(jnp.concatenate([mw[0, 64:128], mw[1, 64:128]], axis=0), part) * scale
        k2[lanes, :] = keys.T.astype(BF16)
        values = dot(jnp.concatenate([mw[0, 128:192], mw[1, 128:192]], axis=0), part) * scale
        vt[0, 0:64, lanes] = values[0:64].astype(BF16)
        vt[1, 0:64, lanes] = values[64:128].astype(BF16)
        if own:
            queries = dot(jnp.concatenate([mw[0, 0:64], mw[1, 0:64]], axis=0), part)
            queries = queries * (scale * (0.125 * math.log2(math.e)))
            qt[0, 0:64, lanes] = queries[0:64].astype(BF16)
            qt[1, 64:128, lanes] = queries[64:128].astype(BF16)
            ht[:, lanes] = dot(hw[...], part)

    def partial_copy(sweep, slot):
        return pltpu.make_async_remote_copy(
            src_ref=pout.at[slot],
            dst_ref=pin.at[sweep, slot],
            send_sem=psend.at[slot],
            recv_sem=precv.at[sweep, slot],
            device_id=along(slot_offset(slot)),
            device_id_type=MESH,
        )

    def scores(index, into):
        block, head = index // 2, index % 2
        into[...] = dot(k2[...], qt[head, :, block * BLOCK : block * BLOCK + BLOCK])

    def attend(index, held):
        head = index % 2
        score = held[...]
        peak = jnp.max(score, axis=0, keepdims=True)
        probs = jnp.exp2(score - peak).astype(BF16)
        result = dot(vt[head], probs)
        return (result[0:64] * (1.0 / result[64:65])).astype(BF16)

    def hand_out(sweep, block, first, second):
        mixed = ht[:, block * BLOCK : block * BLOCK + BLOCK]
        mixed = mixed + jnp.concatenate([first, second], axis=0).astype(F32)
        square = jnp.sum(mixed * mixed, axis=0, keepdims=True)
        gain_column = fgt[:, 0:1]
        share = dot(wot[...], (mixed * gain_column).astype(BF16))
        sq_high = square.astype(BF16).astype(F32)
        tail = jnp.concatenate(
            [sq_high, square - sq_high, jnp.zeros((14, BLOCK), F32)], axis=0
        )
        top = jnp.concatenate([share[0:HALF], tail], axis=0)
        bottom = jnp.concatenate([share[HALF:64], tail], axis=0)
        for pair in range(BLOCK // 128):
            a = top[:, pair * 128 : pair * 128 + 128]
            b = bottom[:, pair * 128 : pair * 128 + 128]
            slot = block * 8 + 2 * pair
            left = jnp.concatenate([a[:, :64], b[:, :64]], axis=1).astype(BF16)
            right = jnp.concatenate([a[:, 64:], b[:, 64:]], axis=1).astype(BF16)
            pout[slot] = left
            partial_copy(sweep, slot).start()
            if slot + 1 < 15:
                pout[slot + 1] = right
                partial_copy(sweep, slot + 1).start()
            else:
                pin[sweep, 15] = right

    def one_sweep(sweep, carry):
        for chunk in range(4):
            project(chunk, chunk < 2)
        scores(0, s0)
        scores(1, s1)
        first = attend(0, s0)
        scores(2, s0)
        second = attend(1, s1)
        hand_out(sweep, 0, first, second)
        scores(3, s1)
        first = attend(2, s0)
        second = attend(3, s1)
        hand_out(sweep, 1, first, second)

        def landed(slot, carry):
            pltpu.make_async_remote_copy(
                src_ref=pout.at[slot], dst_ref=pin.at[sweep, slot],
                send_sem=psend.at[slot], recv_sem=precv.at[sweep, slot],
                device_id=partner, device_id_type=MESH,
            ).wait()
            return carry

        lax.fori_loop(0, 15, landed, 0)
        total = jnp.sum(pin[sweep].astype(F32), axis=0)
        square = total[HALF : HALF + 1] + total[HALF + 1 : HALF + 2]
        scale = lax.rsqrt(square * (1.0 / 2048) + 1e-06)
        own = step_coef * (total[0:HALF] * scale) + noise_coef * noisep[...]
        term[...] = own

        def send_term(later, carry):
            pltpu.make_async_remote_copy(
                src_ref=term, dst_ref=prefix.at[sweep, tm],
                send_sem=tsend.at[later], recv_sem=trecv.at[sweep, tm],
                device_id=(later, sq), device_id_type=MESH,
            ).start()
            return carry

        lax.fori_loop(tm + 1, STEPS, send_term, 0)

        def add_term(earlier, acc):
            pltpu.make_async_remote_copy(
                src_ref=term, dst_ref=prefix.at[sweep, earlier],
                send_sem=tsend.at[earlier], recv_sem=trecv.at[sweep, earlier],
                device_id=(earlier, sq), device_id_type=MESH,
            ).wait_recv()
            return acc + prefix[sweep, earlier]

        before = lax.fori_loop(0, tm, add_term, lsp[...])

        @pl.when(sweep == 0)
        def _():
            gb1[c, 15] = before.astype(BF16)
            gather_start(gb1, 1)
            gather_finish(gb1, 1)
            assemble(gb1, False)

        @pl.when(sweep == 1)
        def _():
            last = before + own
            out_ref[0] = jnp.concatenate([last[:, :64], last[:, 64:]], axis=0).T

        def sent_term(later, carry):
            pltpu.make_async_remote_copy(
                src_ref=term, dst_ref=prefix.at[sweep, tm],
                send_sem=tsend.at[later], recv_sem=trecv.at[sweep, tm],
                device_id=(later, sq), device_id_type=MESH,
            ).wait_send()
            return carry

        lax.fori_loop(tm + 1, STEPS, sent_term, 0)
        return carry

    lax.fori_loop(0, 2, one_sweep, 0)


def body(
    latent_start, noise, step_index, camera_ids, embed_in, time_table, camera_table, norm_gain,
    qkv_weight, final_gain, out_weight, step_sizes, noise_scales,
):
    vmem = pl.BlockSpec(memory_space=pltpu.VMEM)
    smem = pl.BlockSpec(memory_space=pltpu.SMEM)
    tokens = TOK * 2 * CHIPS
    dma = pltpu.SemaphoreType.DMA
    return pl.pallas_call(
        kernel,
        out_shape=jax.ShapeDtypeStruct((1, TOK, 64), F32),
        in_specs=[vmem, vmem, smem] + [vmem] * 8 + [smem, smem],
        out_specs=vmem,
        scratch_shapes=[
            pltpu.VMEM((HALF, 128), F32),
            pltpu.VMEM((HALF, 128), F32),
            pltpu.VMEM((2, 16, 48, 128), BF16),
            pltpu.VMEM((2, 16, HALF, 128), BF16),
            pltpu.VMEM((256, tokens), BF16),
            pltpu.VMEM((2, 192, 256), BF16),
            pltpu.VMEM((128, 256), BF16),
            pltpu.VMEM((64, 256), BF16),
            pltpu.VMEM((16, 2048), F32),
            pltpu.VMEM((16, 128), F32),
            pltpu.VMEM((64, 128), BF16),
            pltpu.VMEM((128, 128), F32),
            pltpu.VMEM((tokens, 128), BF16),
            pltpu.VMEM((2, 80, tokens), BF16),
            pltpu.VMEM((2, 128, tokens // 2), BF16),
            pltpu.VMEM((128, tokens // 2), F32),
            pltpu.VMEM((tokens, BLOCK), F32),
            pltpu.VMEM((tokens, BLOCK), F32),
            pltpu.VMEM((16, 48, 128), BF16),
            pltpu.VMEM((2, 16, 48, 128), BF16),
            pltpu.VMEM((HALF, 128), F32),
            pltpu.VMEM((2, STEPS, HALF, 128), F32),
            dma((2, 16)), dma((2, 16)),
            dma((2, 3)), dma((2, 3)),
            dma, dma,
            dma((16,)), dma((2, 16)),
            dma((16,)), dma((2, 16)),
        ],
        compiler_params=pltpu.CompilerParams(
            collective_id=0, has_side_effects=True, vmem_limit_bytes=56 * 1024 * 1024
        ),
    )(
        latent_start, noise, step_index, camera_ids.reshape(1, TOK), embed_in, time_table,
        camera_table, norm_gain.reshape(1, -1), qkv_weight.reshape(qkv_weight.shape[0], -1),
        final_gain.reshape(1, -1), out_weight, step_sizes, noise_scales,
    )


def solution(mesh):
    in_specs = (
        P("seq", None), P("tm", "seq", None), P("tm"), P("seq"), P(), P(), P(), P(),
        P(None, "seq", None), P(), P(), P(), P(),
    )
    return jax.shard_map(
        body, mesh=mesh, in_specs=in_specs, out_specs=P("tm", "seq", None), check_vma=False
    )
```

time: 332 us -> 87.4 us (0.26)
  waiting for transfers between devices: 197 us -> 0 us
  Pallas kernels: 0 us -> 81.8 us
  blocking collectives: 47.2 us -> 0 us
  matrix products: 34.2 us -> 0 us
  starting transfers between devices: 15.7 us -> 0 us
  between operations: 14.5 us -> 0.74 us
  other arithmetic: 11.1 us -> 0 us
  local copies, waits for them, and re-layouts: 10.1 us -> 4.66 us
    all_gather x2 -> x0, waiting for transfers between devices: 153 us -> none  [body(): lax.all_gather(normed, 'seq', axis=0, tiled=True)]
    pallas_call x0 -> x1, Pallas kernels: none -> 81.8 us  [body(): pl.pallas_call(kernel, out_shape=jax.ShapeDtypeStruct((1, TOK, 64), F32),...]
    all_gather x2 -> x0, blocking collectives: 47.2 us -> none  [entering(): gathered = lax.all_gather(part, axis)]
    all_to_all x2 -> x0, waiting for transfers between devices: 44.1 us -> none  [body(): lax.all_to_all(head_out, 'seq', split_axis=0, concat_axis=1, tiled=True)]
    dot_general x22 -> x0, matrix products: 34.2 us -> none  [the longest x2 12.6 us: body(): jnp.einsum('td,dhk->thk', lax.all_gather(normed, 'seq', axis=0, tiled=Tru...]
    all_to_all x2 -> x0, starting transfers between devices: 15.6 us -> none  [body(): lax.all_to_all(head_out, 'seq', split_axis=0, concat_axis=1, tiled=True)]
    reduce_sum x10 -> x0, other arithmetic: 6.92 us -> none  [the longest x8 6.59 us: one_block(): probs = (expo / jnp.sum(expo, axis=-1, keepdims=True)).astype(jnp.bfloat16)]
  transfers between devices with their start and end apart: 4 -> 0, of which waited for: 4 -> 0; matrix products, arithmetic and copies ran while one was open for 0% -> 0% of each run, Pallas kernels for 0% -> 0%
where the time goes in v1:
time: 87.4 us; the launch traced here: 87.2 us
  Pallas kernels  81.8 us (94%)
  local copies, waits for them, and re-layouts  4.66 us (5%)
    pallas_call x1, Pallas kernels, body(): pl.pallas_call(kernel, out_shape=jax.ShapeDtypeStruct((1, TOK, 64), F32),...  81.8 us
    unnamed x5, local copies, waits for them, and re-layouts  4.66 us

profile of v1, /device:TPU:24, one launch (start us, length us, event | category | flops | bytes accessed | tf_op | source)
XLA Modules:
  0.0 87.2 jit_solution(3811306756332388522)
XLA Ops:
  0.0 0.0 copy-start
  0.7 2.0 %copy.15.wout_ref = bf16[2048,64]{1,0:T(8,128)(2,1)} copy(bf16[2048,64]{0,1:T(8,128)(2,1)} %param.23) | data formatting | bytes 524288 | tf_op args[10]
  2.7 0.0 copy-done
  2.7 1.3 %copy.14 = bf16[2048,1,192]{2,0,1:T(8,128)(2,1)} copy(bf16[2048,1,192]{0,2,1:T(8,128)(2,1)S(1)} %copy-done) | data formatting | bytes 1572864 | tf_op args[8]
  4.0 81.8 %shard_map.127 = f32[1,64,64]{2,1,0:T(8,128)} custom-call(f32[64,64]{1,0:T(8,128)} %ls_ref.1, f32[1,64,64]{2,1,0:T(8,128)} %noise_ref.1, s32[1]{0:T(128)S(6)} %copy.17.step_ref, s32[1,64]{1,0:T(1,128)} %bitcast.7, bf16[64,2048]{1,0:T(8,128)(2,1)} %embed_ref.1, f32[50,2048]{1,0:T(8,128)} %time_ref.1, f32[6,2048]{1,0:T(8,128)} %camt_ref.1, f32[1,2048]{1,0:T(1,128)} %bitcast.5, ...), custom_call_target="tpu_custom_call" | custom-call | tf_op jit(solution)/shard_map/pallas_call | solution.py:379
  85.8 1.4 %copy.18 = f32[1,64,64]{2,1,0:T(8,128)} copy(f32[1,64,64]{2,1,0:T(8,128)} %shard_map.127) | data formatting | bytes 32768
Async XLA Ops:
  0.0 2.7 %copy-start = (bf16[2048,1,192]{0,2,1:T(8,128)(2,1)S(1)}, bf16[2048,1,192]{0,2,1:T(8,128)(2,1)}, u32[]{:S(2)}) copy-start(bf16[2048,1,192]{0,2,1:T(8,128)(2,1)} %param.21) | copy-start | bytes 2359300

commit v2 on v1

--- a/solution.py
+++ b/solution.py
@@ -15,7 +15,7 @@
 HALF = 32
 CHIPS = 16
 STEPS = 16
-BLOCK = 512
+BLOCK = 256
 RELAYS = ((9, 16), (3, 9), (0, 3))
 
 
@@ -54,12 +54,14 @@
 
 
 def kernel(
-    ls_ref, noise_ref, step_ref, cam_ref, embed_ref, time_ref, camt_ref, ngain_ref, w_ref,
-    fgain_ref, wout_ref, sizes_ref, scales_ref,
+    ls_ref, noise_hbm, step_ref, cam_ref, embed_hbm, time_hbm, camt_hbm, ngain_hbm, w_hbm,
+    fgain_hbm, wout_hbm, sizes_ref, scales_ref,
     out_ref,
-    lsp, noisep, gb0, gb1, u, mw, hw, gw, table, ncol, wot, fgt, k2, vt, qt, ht, s0, s1,
-    pout, pin, term, prefix,
-    gsend, grecv, rsend, rrecv, msend, mrecv, psend, precv, tsend, trecv,
+    noise_ref, embed_ref, time_ref, camt_ref, ngain_ref, w_ref, fgain_ref, loaded,
+    lsp, noisep, gb, cams, u, mw, hw, gw, table, ncol, wot, fgt, k2, vt, qt, ht, s0, s1,
+    pout, pin, qout, qin, term, prefix,
+    gsend, grecv, rsend, rrecv, csend, crecv, ksend, krecv, msend, mrecv,
+    psend, precv, qsend, qrecv, tsend, trecv,
 ):
     tm, sq = lax.axis_index("tm"), lax.axis_index("seq")
     z, c = sq // 2, sq % 2
@@ -85,83 +87,100 @@
     lax.fori_loop(1, STEPS, greet_tm, 0)
     pl.semaphore_signal(barrier, inc=1, device_id=partner, device_id_type=MESH)
 
+    columns = pl.ds(pl.multiple_of(z * 128, 128), 128)
+    loads = [
+        pltpu.make_async_copy(source, target, loaded.at[index])
+        for index, (source, target) in enumerate(
+            (
+                (time_hbm, time_ref), (camt_hbm, camt_ref), (embed_hbm, embed_ref),
+                (ngain_hbm, ngain_ref), (w_hbm, w_ref), (noise_hbm, noise_ref),
+                (fgain_hbm.at[:, columns], fgain_ref), (wout_hbm.at[:, columns], wot),
+            )
+        )
+    ]
+    for load in loads:
+        load.start()
+
     lsp[...] = pack(ls_ref[...])
-    gb0[c, 15, 0:HALF, :] = lsp[...].astype(BF16)
-    cam = cam_ref[...].astype(F32).astype(BF16)
-    gb0[c, 15, HALF:48, :] = jnp.broadcast_to(jnp.concatenate([cam, cam], axis=1), (16, 128))
+    gb[0, c, 15] = lsp[...].astype(BF16)
+    cam = cam_ref[...].astype(F32)
+    cams[c, 15] = jnp.concatenate([cam, cam], axis=1)
 
     pl.semaphore_wait(barrier, CHIPS - 1 + STEPS - 1 + 1)
 
-    def gather_copy(buf, phase, slot):
+    def gather_copy(buf, send, recv, slot, into):
         return pltpu.make_async_remote_copy(
             src_ref=buf.at[c, 15],
-            dst_ref=buf.at[c, mirror(slot)],
-            send_sem=gsend.at[phase, slot],
-            recv_sem=grecv.at[phase, mirror(slot)],
+            dst_ref=buf.at[c, into],
+            send_sem=send.at[slot],
+            recv_sem=recv.at[into],
             device_id=along(slot_offset(slot)),
             device_id_type=MESH,
         )
 
-    def gather_wait(buf, phase, slot):
-        return pltpu.make_async_remote_copy(
-            src_ref=buf.at[c, 15],
-            dst_ref=buf.at[c, slot],
-            send_sem=gsend.at[phase, slot],
-            recv_sem=grecv.at[phase, slot],
-            device_id=along(slot_offset(slot)),
-            device_id_type=MESH,
-        )
-
-    def relay_copy(buf, phase, index, core):
+    def relay_copy(buf, send, recv, index, core):
         first, last = RELAYS[index]
         part = buf.at[core, pl.ds(first, last - first)]
         return pltpu.make_async_remote_copy(
             src_ref=part,
             dst_ref=part,
-            send_sem=rsend.at[phase, index],
-            recv_sem=rrecv.at[phase, index],
+            send_sem=send.at[index],
+            recv_sem=recv.at[index],
             device_id=partner,
             device_id_type=MESH,
         )
 
-    def gather_start(buf, phase):
+    latents = [
+        (gb.at[phase], gsend.at[phase], grecv.at[phase], rsend.at[phase], rrecv.at[phase])
+        for phase in range(2)
+    ]
+    cameras = (cams, csend, crecv, ksend, krecv)
+
+    def gather_start(*arrays):
         for slot in range(15):
-            gather_copy(buf, phase, slot).start()
-
-    def gather_finish(buf, phase):
+            for buf, send, recv, _, _ in arrays:
+                gather_copy(buf, send, recv, slot, mirror(slot)).start()
+
+    def gather_finish(*arrays):
         for index, (first, last) in enumerate(RELAYS):
-            for slot in reversed(range(first, min(last, 15))):
-                gather_wait(buf, phase, slot).wait_recv()
-            relay_copy(buf, phase, index, c).start()
+            for buf, send, recv, again, landing in arrays:
+                for slot in reversed(range(first, min(last, 15))):
+                    gather_copy(buf, send, recv, slot, slot).wait_recv()
+                relay_copy(buf, again, landing, index, c).start()
         for index in range(len(RELAYS)):
-            relay_copy(buf, phase, index, other).wait_recv()
-        for slot in range(15):
-            gather_copy(buf, phase, slot).wait_send()
-        for index in range(len(RELAYS)):
-            relay_copy(buf, phase, index, c).wait_send()
-
-    def assemble(buf, cameras):
+            for buf, _, _, again, landing in arrays:
+                relay_copy(buf, again, landing, index, other).wait_recv()
+        for buf, send, recv, again, landing in arrays:
+            for slot in range(15):
+                gather_copy(buf, send, recv, slot, mirror(slot)).wait_send()
+            for index in range(len(RELAYS)):
+                relay_copy(buf, again, landing, index, c).wait_send()
+
+    def assemble(phase):
         for side in range(2):
             core = c if side == 0 else other
             for pair in range(8):
                 lanes = slice(side * 1024 + pair * 128, side * 1024 + pair * 128 + 128)
-                left = buf[core, 2 * pair]
-                right = buf[core, 2 * pair + 1]
+                left = gb[phase, core, 2 * pair]
+                right = gb[phase, core, 2 * pair + 1]
                 low = jnp.concatenate([left[:, :64], right[:, :64]], axis=1)
                 high = jnp.concatenate([left[:, 64:], right[:, 64:]], axis=1)
-                tile = jnp.concatenate([low[:HALF], high[:HALF]], axis=0)
+                tile = jnp.concatenate([low, high], axis=0)
                 u[0:64, lanes] = tile
                 u[64:128, lanes] = tile
                 u[128:192, lanes] = tile
-                if cameras:
-                    ids = low[HALF : HALF + 16].astype(F32)
+                if phase == 0:
+                    near = lax.broadcasted_iota(jnp.int32, (1, 128), 1) < 64
+                    ids = jnp.where(near, cams[core, 2 * pair], cams[core, 2 * pair + 1])
                     row = lax.broadcasted_iota(jnp.int32, (16, 128), 0).astype(F32)
                     one = jnp.where(ids == row, 1.0, 0.0).astype(BF16)
                     u[192:208, lanes] = one
                     u[208:224, lanes] = one
                     u[224:240, lanes] = one
 
-    gather_start(gb0, 0)
+    gather_start(latents[0], cameras)
+    for load in loads:
+        load.wait()
 
     tau = step_ref[0]
     rows = camt_ref[...] + time_ref[pl.ds(tau, 1), :]
@@ -171,7 +190,7 @@
     gain = ngain_ref[...]
     eg_high, eg_low = split2(embed.astype(F32) * gain)
     rg_high, rg_low = split2(rows * gain)
-    folded = dot(jnp.concatenate([eg_high, rg_high, eg_low, rg_low], axis=0), w_ref[...])
+    folded = dot_nt(jnp.concatenate([eg_high, rg_high, eg_low, rg_low], axis=0), w_ref[...])
     fold_x = folded[0:64] + folded[80:144]
     fold_e = folded[64:80] + folded[144:160]
     fx_high = fold_x.astype(BF16).astype(F32)
@@ -199,7 +218,6 @@
     gw[...] = jnp.concatenate(g3 + c3 + [jnp.zeros((16, 64), F32)], axis=0).T.astype(BF16)
     ncol[...] = jnp.broadcast_to(jnp.sum(rows * rows, axis=1, keepdims=True), ncol.shape)
 
-    columns = pl.ds(pl.multiple_of(z * 128, 128), 128)
     h3 = [part.astype(F32) for part in split3(table[:, columns])]
     hw[...] = jnp.concatenate(
         [embed_ref[:, columns].astype(F32), jnp.zeros((128, 128), F32)]
@@ -207,8 +225,7 @@
         + [jnp.zeros((16, 128), F32)],
         axis=0,
     ).T.astype(BF16)
-    fgt[...] = jnp.broadcast_to(fgain_ref[:, columns], (128, 128)).T
-    wot[...] = wout_ref[columns, :].astype(F32).T.astype(BF16)
+    fgt[...] = jnp.broadcast_to(fgain_ref[...], (128, 128)).T
     noisep[...] = pack(noise_ref[0])
     step_coef = sizes_ref[tau]
     noise_coef = scales_ref[tau]
@@ -222,11 +239,11 @@
         src_ref=mw.at[other], dst_ref=mw.at[other], send_sem=msend, recv_sem=mrecv,
         device_id=partner, device_id_type=MESH,
     ).wait_recv()
-    gather_finish(gb0, 0)
-    assemble(gb0, True)
+    gather_finish(latents[0], cameras)
+    assemble(0)
 
     def project(chunk, own):
-        lanes = slice(chunk * BLOCK, chunk * BLOCK + BLOCK)
+        lanes = slice(chunk * 512, chunk * 512 + 512)
         part = u[:, lanes]
         mixed = dot(gw[...], part)
         square = jnp.sum(mixed * part[0:64].astype(F32), axis=0, keepdims=True)
@@ -245,15 +262,20 @@
             qt[1, 64:128, lanes] = queries[64:128].astype(BF16)
             ht[:, lanes] = dot(hw[...], part)
 
-    def partial_copy(sweep, slot):
-        return pltpu.make_async_remote_copy(
-            src_ref=pout.at[slot],
-            dst_ref=pin.at[sweep, slot],
-            send_sem=psend.at[slot],
-            recv_sem=precv.at[sweep, slot],
-            device_id=along(slot_offset(slot)),
-            device_id_type=MESH,
-        )
+    def partial_copies(sweep, slot):
+        return [
+            pltpu.make_async_remote_copy(
+                src_ref=source.at[slot],
+                dst_ref=target.at[sweep, slot],
+                send_sem=send.at[slot],
+                recv_sem=recv.at[sweep, slot],
+                device_id=along(slot_offset(slot)),
+                device_id_type=MESH,
+            )
+            for source, target, send, recv in (
+                (pout, pin, psend, precv), (qout, qin, qsend, qrecv)
+            )
+        ]
 
     def scores(index, into):
         block, head = index // 2, index % 2
@@ -271,55 +293,52 @@
         mixed = ht[:, block * BLOCK : block * BLOCK + BLOCK]
         mixed = mixed + jnp.concatenate([first, second], axis=0).astype(F32)
         square = jnp.sum(mixed * mixed, axis=0, keepdims=True)
-        gain_column = fgt[:, 0:1]
-        share = dot(wot[...], (mixed * gain_column).astype(BF16))
-        sq_high = square.astype(BF16).astype(F32)
-        tail = jnp.concatenate(
-            [sq_high, square - sq_high, jnp.zeros((14, BLOCK), F32)], axis=0
+        high, low = split2(mixed * fgt[:, 0:1])
+        weight = wot[...]
+        share = dot(
+            jnp.concatenate([weight, weight], axis=1), jnp.concatenate([high, low], axis=0)
         )
-        top = jnp.concatenate([share[0:HALF], tail], axis=0)
-        bottom = jnp.concatenate([share[HALF:64], tail], axis=0)
         for pair in range(BLOCK // 128):
-            a = top[:, pair * 128 : pair * 128 + 128]
-            b = bottom[:, pair * 128 : pair * 128 + 128]
-            slot = block * 8 + 2 * pair
-            left = jnp.concatenate([a[:, :64], b[:, :64]], axis=1).astype(BF16)
-            right = jnp.concatenate([a[:, 64:], b[:, 64:]], axis=1).astype(BF16)
-            pout[slot] = left
-            partial_copy(sweep, slot).start()
-            if slot + 1 < 15:
-                pout[slot + 1] = right
-                partial_copy(sweep, slot + 1).start()
-            else:
-                pin[sweep, 15] = right
+            lanes = slice(pair * 128, pair * 128 + 128)
+            a, b, s = share[0:HALF, lanes], share[HALF:64, lanes], square[:, lanes]
+            for side in range(2):
+                slot = block * (BLOCK // TOK) + 2 * pair + side
+                half = slice(64 * side, 64 * side + 64)
+                packed = jnp.concatenate([a[:, half], b[:, half]], axis=1).astype(BF16)
+                squares = jnp.concatenate([s[:, half], s[:, half]], axis=1)
+                if slot < 15:
+                    pout[slot] = packed
+                    qout[slot] = squares
+                    for copy in partial_copies(sweep, slot):
+                        copy.start()
+                else:
+                    pin[sweep, 15] = packed
+                    qin[sweep, 15] = squares
 
     def one_sweep(sweep, carry):
         for chunk in range(4):
             project(chunk, chunk < 2)
+        held = (s0, s1)
+        steps = 2 * (1024 // BLOCK)
         scores(0, s0)
-        scores(1, s1)
-        first = attend(0, s0)
-        scores(2, s0)
-        second = attend(1, s1)
-        hand_out(sweep, 0, first, second)
-        scores(3, s1)
-        first = attend(2, s0)
-        second = attend(3, s1)
-        hand_out(sweep, 1, first, second)
+        results = []
+        for index in range(steps):
+            if index + 1 < steps:
+                scores(index + 1, held[(index + 1) % 2])
+            results.append(attend(index, held[index % 2]))
+            if index % 2:
+                hand_out(sweep, index // 2, results[index - 1], results[index])
 
         def landed(slot, carry):
-            pltpu.make_async_remote_copy(
-                src_ref=pout.at[slot], dst_ref=pin.at[sweep, slot],
-                send_sem=psend.at[slot], recv_sem=precv.at[sweep, slot],
-                device_id=partner, device_id_type=MESH,
-            ).wait()
+            for copy in partial_copies(sweep, slot):
+                copy.wait()
             return carry
 
         lax.fori_loop(0, 15, landed, 0)
         total = jnp.sum(pin[sweep].astype(F32), axis=0)
-        square = total[HALF : HALF + 1] + total[HALF + 1 : HALF + 2]
+        square = jnp.sum(qin[sweep], axis=0)
         scale = lax.rsqrt(square * (1.0 / 2048) + 1e-06)
-        own = step_coef * (total[0:HALF] * scale) + noise_coef * noisep[...]
+        own = step_coef * (total * scale) + noise_coef * noisep[...]
         term[...] = own
 
         def send_term(later, carry):
@@ -344,10 +363,10 @@
 
         @pl.when(sweep == 0)
         def _():
-            gb1[c, 15] = before.astype(BF16)
-            gather_start(gb1, 1)
-            gather_finish(gb1, 1)
-            assemble(gb1, False)
+            gb[1, c, 15] = before.astype(BF16)
+            gather_start(latents[1])
+            gather_finish(latents[1])
+            assemble(1)
 
         @pl.when(sweep == 1)
         def _():
@@ -374,18 +393,27 @@
 ):
     vmem = pl.BlockSpec(memory_space=pltpu.VMEM)
     smem = pl.BlockSpec(memory_space=pltpu.SMEM)
+    hbm = pl.BlockSpec(memory_space=pl.ANY)
     tokens = TOK * 2 * CHIPS
     dma = pltpu.SemaphoreType.DMA
     return pl.pallas_call(
         kernel,
         out_shape=jax.ShapeDtypeStruct((1, TOK, 64), F32),
-        in_specs=[vmem, vmem, smem] + [vmem] * 8 + [smem, smem],
+        in_specs=[vmem, hbm, smem, vmem] + [hbm] * 7 + [smem, smem],
         out_specs=vmem,
         scratch_shapes=[
+            pltpu.VMEM((1, TOK, 64), F32),
+            pltpu.VMEM((64, 2048), BF16),
+            pltpu.VMEM((50, 2048), F32),
+            pltpu.VMEM((6, 2048), F32),
+            pltpu.VMEM((1, 2048), F32),
+            pltpu.VMEM((192, 2048), BF16),
+            pltpu.VMEM((1, 128), F32),
+            dma((8,)),
             pltpu.VMEM((HALF, 128), F32),
             pltpu.VMEM((HALF, 128), F32),
-            pltpu.VMEM((2, 16, 48, 128), BF16),
-            pltpu.VMEM((2, 16, HALF, 128), BF16),
+            pltpu.VMEM((2, 2, 16, HALF, 128), BF16),
+            pltpu.VMEM((2, 16, 1, 128), F32),
             pltpu.VMEM((256, tokens), BF16),
             pltpu.VMEM((2, 192, 256), BF16),
             pltpu.VMEM((128, 256), BF16),
@@ -400,13 +428,18 @@
             pltpu.VMEM((128, tokens // 2), F32),
             pltpu.VMEM((tokens, BLOCK), F32),
             pltpu.VMEM((tokens, BLOCK), F32),
-            pltpu.VMEM((16, 48, 128), BF16),
-            pltpu.VMEM((2, 16, 48, 128), BF16),
+            pltpu.VMEM((16, HALF, 128), BF16),
+            pltpu.VMEM((2, 16, HALF, 128), BF16),
+            pltpu.VMEM((16, 1, 128), F32),
+            pltpu.VMEM((2, 16, 1, 128), F32),
             pltpu.VMEM((HALF, 128), F32),
             pltpu.VMEM((2, STEPS, HALF, 128), F32),
             dma((2, 16)), dma((2, 16)),
             dma((2, 3)), dma((2, 3)),
+            dma((16,)), dma((16,)),
+            dma((3,)), dma((3,)),
             dma, dma,
+            dma((16,)), dma((2, 16)),
             dma((16,)), dma((2, 16)),
             dma((16,)), dma((2, 16)),
         ],
@@ -415,8 +448,8 @@
         ),
     )(
         latent_start, noise, step_index, camera_ids.reshape(1, TOK), embed_in, time_table,
-        camera_table, norm_gain.reshape(1, -1), qkv_weight.reshape(qkv_weight.shape[0], -1),
-        final_gain.reshape(1, -1), out_weight, step_sizes, noise_scales,
+        camera_table, norm_gain.reshape(1, -1), jnp.transpose(qkv_weight, (1, 2, 0)).reshape(-1, qkv_weight.shape[0]),
+        final_gain.reshape(1, -1), out_weight.T, step_sizes, noise_scales,
     )
 
 

time: 87.4 us -> 75.3 us (0.86)
  Pallas kernels: 81.8 us -> 73 us
  local copies, waits for them, and re-layouts: 4.66 us -> 1.38 us
    pallas_call x1, Pallas kernels: 81.8 us -> 73 us  [body(): pl.pallas_call(kernel, out_shape=jax.ShapeDtypeStruct((1, TOK, 64), F32),...]
    unnamed x5 -> x1, local copies, waits for them, and re-layouts: 4.66 us -> 1.38 us
where the time goes in v2:
time: 75.3 us; the launch traced here: 75 us
  Pallas kernels  73 us (97%)
  local copies, waits for them, and re-layouts  1.38 us (2%)
    pallas_call x1, Pallas kernels, body(): pl.pallas_call(kernel, out_shape=jax.ShapeDtypeStruct((1, TOK, 64), F32),...  73 us

profile of v2, /device:TPU:24, one launch (start us, length us, event | category | flops | bytes accessed | tf_op | source)
XLA Modules:
  0.0 75.0 jit_solution(18347488378295194130)
XLA Ops:
  0.7 73.0 %shard_map.127 = f32[1,64,64]{2,1,0:T(8,128)} custom-call(f32[64,64]{1,0:T(8,128)} %ls_ref.1, f32[1,64,64]{2,1,0:T(8,128)} %noise_hbm.1, s32[1]{0:T(128)S(6)} %copy.15.step_ref, s32[1,64]{1,0:T(1,128)} %bitcast.11, bf16[64,2048]{1,0:T(8,128)(2,1)} %embed_hbm.1, f32[50,2048]{1,0:T(8,128)} %time_hbm.1, f32[6,2048]{1,0:T(8,128)} %camt_hbm.1, ...), custom_call_target="tpu_custom_call" | custom-call | tf_op jit(solution)/shard_map/pallas_call | solution.py:399
  73.7 1.4 %copy.16 = f32[1,64,64]{2,1,0:T(8,128)} copy(f32[1,64,64]{2,1,0:T(8,128)} %shard_map.127) | data formatting | bytes 32768

commit v3 on v2

--- a/solution.py
+++ b/solution.py
@@ -150,11 +150,12 @@
         for index in range(len(RELAYS)):
             for buf, _, _, again, landing in arrays:
                 relay_copy(buf, again, landing, index, other).wait_recv()
-        for buf, send, recv, again, landing in arrays:
-            for slot in range(15):
-                gather_copy(buf, send, recv, slot, mirror(slot)).wait_send()
-            for index in range(len(RELAYS)):
-                relay_copy(buf, again, landing, index, c).wait_send()
+
+    def gather_sent(buf, send, recv, again, landing):
+        for slot in range(15):
+            gather_copy(buf, send, recv, slot, mirror(slot)).wait_send()
+        for index in range(len(RELAYS)):
+            relay_copy(buf, again, landing, index, c).wait_send()
 
     def assemble(phase):
         for side in range(2):
@@ -329,12 +330,17 @@
             if index % 2:
                 hand_out(sweep, index // 2, results[index - 1], results[index])
 
-        def landed(slot, carry):
+        gather_sent(
+            gb.at[sweep], gsend.at[sweep], grecv.at[sweep], rsend.at[sweep], rrecv.at[sweep]
+        )
+
+        @pl.when(sweep == 0)
+        def _():
+            gather_sent(*cameras)
+
+        for slot in range(15):
             for copy in partial_copies(sweep, slot):
-                copy.wait()
-            return carry
-
-        lax.fori_loop(0, 15, landed, 0)
+                copy.wait_recv()
         total = jnp.sum(pin[sweep].astype(F32), axis=0)
         square = jnp.sum(qin[sweep], axis=0)
         scale = lax.rsqrt(square * (1.0 / 2048) + 1e-06)
@@ -351,6 +357,18 @@
 
         lax.fori_loop(tm + 1, STEPS, send_term, 0)
 
+        for slot in range(15):
+            for copy in partial_copies(sweep, slot):
+                copy.wait_send()
+
+        def sent_term(later, carry):
+            pltpu.make_async_remote_copy(
+                src_ref=term, dst_ref=prefix.at[sweep, tm],
+                send_sem=tsend.at[later], recv_sem=trecv.at[sweep, tm],
+                device_id=(later, sq), device_id_type=MESH,
+            ).wait_send()
+            return carry
+
         def add_term(earlier, acc):
             pltpu.make_async_remote_copy(
                 src_ref=term, dst_ref=prefix.at[sweep, earlier],
@@ -365,6 +383,7 @@
         def _():
             gb[1, c, 15] = before.astype(BF16)
             gather_start(latents[1])
+            lax.fori_loop(tm + 1, STEPS, sent_term, 0)
             gather_finish(latents[1])
             assemble(1)
 
@@ -372,16 +391,8 @@
         def _():
             last = before + own
             out_ref[0] = jnp.concatenate([last[:, :64], last[:, 64:]], axis=0).T
-
-        def sent_term(later, carry):
-            pltpu.make_async_remote_copy(
-                src_ref=term, dst_ref=prefix.at[sweep, tm],
-                send_sem=tsend.at[later], recv_sem=trecv.at[sweep, tm],
-                device_id=(later, sq), device_id_type=MESH,
-            ).wait_send()
-            return carry
-
-        lax.fori_loop(tm + 1, STEPS, sent_term, 0)
+            lax.fori_loop(tm + 1, STEPS, sent_term, 0)
+
         return carry
 
     lax.fori_loop(0, 2, one_sweep, 0)

time: 75.3 us -> 75.1 us (level)
  no operation moved by 1% of the time
where the time goes in v3:
time: 75.1 us; the launch traced here: 74.6 us
  Pallas kernels  72.6 us (97%)
  local copies, waits for them, and re-layouts  1.38 us (2%)
    pallas_call x1, Pallas kernels, body(): pl.pallas_call(kernel, out_shape=jax.ShapeDtypeStruct((1, TOK, 64), F32),...  72.6 us

profile of v3, /device:TPU:24, one launch (start us, length us, event | category | flops | bytes accessed | tf_op | source)
XLA Modules:
  0.0 74.6 jit_solution(11319982087000232933)
XLA Ops:
  0.7 72.6 %shard_map.127 = f32[1,64,64]{2,1,0:T(8,128)} custom-call(f32[64,64]{1,0:T(8,128)} %ls_ref.1, f32[1,64,64]{2,1,0:T(8,128)} %noise_hbm.1, s32[1]{0:T(128)S(6)} %copy.15.step_ref, s32[1,64]{1,0:T(1,128)} %bitcast.11, bf16[64,2048]{1,0:T(8,128)(2,1)} %embed_hbm.1, f32[50,2048]{1,0:T(8,128)} %time_hbm.1, f32[6,2048]{1,0:T(8,128)} %camt_hbm.1, ...), custom_call_target="tpu_custom_call" | custom-call | tf_op jit(solution)/shard_map/pallas_call | solution.py:410
  73.2 1.4 %copy.16 = f32[1,64,64]{2,1,0:T(8,128)} copy(f32[1,64,64]{2,1,0:T(8,128)} %shard_map.127) | data formatting | bytes 32768

commit v4 on v3

--- a/solution.py
+++ b/solution.py
@@ -142,8 +142,8 @@
                 gather_copy(buf, send, recv, slot, mirror(slot)).start()
 
     def gather_finish(*arrays):
-        for index, (first, last) in enumerate(RELAYS):
-            for buf, send, recv, again, landing in arrays:
+        for buf, send, recv, again, landing in arrays:
+            for index, (first, last) in enumerate(RELAYS):
                 for slot in reversed(range(first, min(last, 15))):
                     gather_copy(buf, send, recv, slot, slot).wait_recv()
                 relay_copy(buf, again, landing, index, c).start()

time: 75.1 us -> 74.6 us (level)
  no operation moved by 1% of the time
where the time goes in v4:
time: 74.6 us; the launch traced here: 74.3 us
  Pallas kernels  72.3 us (97%)
  local copies, waits for them, and re-layouts  1.38 us (2%)
    pallas_call x1, Pallas kernels, body(): pl.pallas_call(kernel, out_shape=jax.ShapeDtypeStruct((1, TOK, 64), F32),...  72.3 us

profile of v4, /device:TPU:24, one launch (start us, length us, event | category | flops | bytes accessed | tf_op | source)
XLA Modules:
  0.0 74.3 jit_solution(12791754192215371559)
XLA Ops:
  0.7 72.3 %shard_map.127 = f32[1,64,64]{2,1,0:T(8,128)} custom-call(f32[64,64]{1,0:T(8,128)} %ls_ref.1, f32[1,64,64]{2,1,0:T(8,128)} %noise_hbm.1, s32[1]{0:T(128)S(6)} %copy.15.step_ref, s32[1,64]{1,0:T(1,128)} %bitcast.11, bf16[64,2048]{1,0:T(8,128)(2,1)} %embed_hbm.1, f32[50,2048]{1,0:T(8,128)} %time_hbm.1, f32[6,2048]{1,0:T(8,128)} %camt_hbm.1, ...), custom_call_target="tpu_custom_call" | custom-call | tf_op jit(solution)/shard_map/pallas_call | solution.py:410
  72.9 1.4 %copy.16 = f32[1,64,64]{2,1,0:T(8,128)} copy(f32[1,64,64]{2,1,0:T(8,128)} %shard_map.127) | data formatting | bytes 32768
